TPU v7x, 32 devices: a whole 2x2x4 slice. The times are simulated.
32 devices in a mesh: cases: 2 (over y), tm: 4 (over z), region: 4 (over x, core).
Axes of the slice: x: 2, y: 2, z: 4, core: 2. Of those that a mesh axis runs over, the one named last changes fastest.
Arguments:
- former_estimate: float32 [384, 32, 128], P(('cases', 'tm'), 'region'), parts along dimension 0, may hold values from -6 to 6
- excitation: bfloat16 [384, 32, 128], P(('cases', 'tm'), 'region'), parts along dimension 0, may hold values from -6 to 6
- susceptance_maps: bfloat16 [32, 4, 128, 128], P('region'), may hold values from -0.125 to 0.125
- linked_partner_target: int32 [32, 4], P('region'), may hold values from 0 to 31, as said below
- attenuation: float32 [32, 64], P('region'), may hold values from 0.0002 to 0.03
- revolution_angle: float32 [32, 64], P('region'), may hold values from -0.6 to 0.6
- saturated_flag: int32 [64, 64], P(('cases', 'region')), parts along dimension 0, may hold values 0 or 1
- gain_surge: float32 [384], P(('cases', 'tm')), parts along dimension 0, may hold values from 0.25 to 1
Outputs:
- waveform: float32 [384, 32, 128], P(('cases', 'tm'), 'region'), parts along dimension 0
There are 2 independent parts, one for each index of `cases`. A program takes and returns all parts, laid end to end along the dimension named above; an argument that names none is the same for every part. Nothing has to cross between parts.
Inputs may be any that keep to these rules, and one draw needn't show every extreme that they name: `linked_partner_target`: block row b lies in region g = b // 8. Its column 0 is b itself, column 1 a block of region g, column 2 one of the last 4 blocks of region g - 1 and column 3 one of the first 4 blocks of region g + 1, regions counted around a cycle of 32 // 8.
All inputs are finite; a program needn't handle non-finite values. No bound on the sum of `saturated_flag` on one device may be relied on, other than what follows from the above.
Results may differ from a plain program's by a relative error of at most 0.0017.
Values may be sent and summed in bfloat16 or wider, within the bound.
A program may use at most 64 MiB of HBM per device.

v0:
```python
import jax
import jax.numpy as jnp
from jax import lax
from jax.sharding import PartitionSpec as P

BND = 4
SWEEPS = 3
clip_level = 0.5


def with_halo(block, sides, width):
    for axis, dim in sides:
        count = lax.axis_size(axis)
        forward = [(i, i + 1) for i in range(count - 1)]
        forward.append((count - 1, 0))
        backward = [(target, source) for source, target in forward]
        low = lax.ppermute(
            lax.slice_in_dim(block, block.shape[dim] - width, None, axis=dim), axis, forward
        )
        high = lax.ppermute(lax.slice_in_dim(block, 0, width, axis=dim), axis, backward)
        block = jnp.concatenate([low, block, high], axis=dim)
    return block


def complex_mul(first, second):
    half = first.shape[-1] // 2
    first_re, first_im = (first[..., :half], first[..., half:])
    second_re, second_im = (second[..., :half], second[..., half:])
    return jnp.concatenate(
        [first_re * second_re - first_im * second_im, first_re * second_im + first_im * second_re],
        axis=-1,
    )


def combine(early, late):
    return (complex_mul(late[0], early[0]), complex_mul(late[0], early[1]) + late[1])


def bus_terms(attenuation, revolution_angle):
    modulus = jnp.exp(-attenuation)
    cosine = modulus * jnp.cos(revolution_angle)
    sine = modulus * jnp.sin(revolution_angle)
    argument_spin = jnp.concatenate([cosine, sine], axis=-1)
    input_gain = jnp.sqrt((1.0 - cosine) ** 2 + sine**2)
    return (argument_spin, jnp.concatenate([input_gain, input_gain], axis=-1))


def limit_current(current, saturated_flag):
    half = current.shape[-1] // 2
    square = current[..., :half] ** 2 + current[..., half:] ** 2
    scaling_factor = jnp.where(
        saturated_flag == 1, clip_level / jnp.sqrt(clip_level**2 + square), 1.0
    )
    return current * jnp.concatenate([scaling_factor, scaling_factor], axis=-1)


def periodic_end(total_a, total_b):
    half = total_a.shape[-1] // 2
    denom_re = 1.0 - total_a[..., :half]
    denom_im = -total_a[..., half:]
    square = denom_re**2 + denom_im**2
    conjugate = jnp.concatenate([denom_re / square, -denom_im / square], axis=-1)
    return complex_mul(total_b, conjugate)


def local(
    former_estimate,
    excitation,
    susceptance_maps,
    linked_partner_target,
    attenuation,
    revolution_angle,
    saturated_flag,
    gain_surge,
):
    blocks = former_estimate.shape[1]
    buses = attenuation.shape[1]
    argument_spin, input_gain = bus_terms(attenuation, revolution_angle)
    incremental_spin = gain_surge[:, None, None] * argument_spin[None]
    drive_base = excitation.astype(jnp.float32)
    region_index = lax.axis_index("region")
    network = blocks * lax.axis_size("region")
    local_col = (linked_partner_target - region_index * blocks) % network
    local_col = jnp.where(local_col >= network - BND, local_col - network, local_col) + BND
    unit = jnp.concatenate(
        [jnp.ones((blocks, buses), jnp.float32), jnp.zeros((blocks, buses), jnp.float32)], axis=-1
    )
    nothing = jnp.zeros((blocks, 2 * buses), jnp.float32)
    wave = former_estimate
    for sweep_index in range(SWEEPS):
        rounded = wave.astype(jnp.bfloat16)
        extended = with_halo(rounded, (("region", 1),), BND)
        picked = extended[:, local_col, :]
        current = jnp.einsum(
            "tbkj,bkij->tbi", picked, susceptance_maps, preferred_element_type=jnp.float32
        )
        drive = input_gain[None] * (drive_base - limit_current(current, saturated_flag[None]))
        local_a, local_b = lax.associative_scan(combine, (incremental_spin, drive), axis=0)
        own_map = (local_a[-1], local_b[-1])
        every_a, every_b = (
            lax.all_gather(own_map[0][None], "tm", axis=0, tiled=True),
            lax.all_gather(own_map[1][None], "tm", axis=0, tiled=True),
        )
        run_a, run_b = lax.associative_scan(combine, (every_a, every_b), axis=0)
        total_a, total_b = (run_a[-1], run_b[-1])
        time_index = lax.axis_index("tm")
        earlier = jnp.maximum(time_index - 1, 0)
        prior_a = lax.dynamic_index_in_dim(run_a, earlier, 0, keepdims=False)
        prior_b = lax.dynamic_index_in_dim(run_b, earlier, 0, keepdims=False)
        before = (
            jnp.where(time_index > 0, prior_a, unit),
            jnp.where(time_index > 0, prior_b, nothing),
        )
        end_state = periodic_end(total_a, total_b)
        start_state = complex_mul(before[0], end_state) + before[1]
        wave = complex_mul(local_a, start_state[None]) + local_b
    return wave


def solution(mesh):
    in_specs = (
        P(("cases", "tm"), "region", None),
        P(("cases", "tm"), "region", None),
        P("region", None, None, None),
        P("region", None),
        P("region", None),
        P("region", None),
        P(("cases", "region"), None),
        P(("cases", "tm")),
    )
    out_specs = P(("cases", "tm"), "region", None)
    return jax.shard_map(local, mesh=mesh, in_specs=in_specs, out_specs=out_specs, check_vma=False)
```

profile of v0, /device:TPU:0, one launch (start us, length us, event | category | flops | bytes accessed | tf_op | source)
XLA Modules:
  0.0 90.0 jit_solution(5454847663768018754)
XLA Ops:
  0.0 1.1 %copy.114 = bf16[48,8,128]{2,0,1:T(8,128)(2,1)S(1)} copy(f32[48,8,128]{2,1,0:T(8,128)} %param.8) | data formatting | bytes 294912 | tf_op args[0]
  1.1 0.5 collective-permute-start
  1.6 2.0 %collective-permute-start.1 = (bf16[48,4,128]{2,0,1:T(8,128)(2,1)S(1)}, bf16[48,4,128]{2,0,1:T(8,128)(2,1)S(1)}, u32[]{:S(2)}, u32[]{:S(2)}) collective-permute-start(bf16[48,4,128]{2,0,1:T(8,128)(2,1)S(1)} %get-tuple-element.68), channel_id=1, source_target_pairs={{1,0},{2,1},{3,2},{0,3},{5,4},{6,5},{7,6},{4,7},{9,8},{10,9},{11,1... | collective-permute-start | bytes 147464 | tf_op jit(solution)/shard_map/ppermute | solution.py:20
  3.6 0.7 copy-done.9
  4.5 0.5 copy-done.5
  5.1 0.7 copy-done.10
  5.9 0.6 copy-done.1
  6.6 0.6 gather_fusion
  7.3 0.5 convolution_bitcast_fusion.2
  8.0 0.7 copy-done.2
  12.4 0.5 slice-done
  13.0 0.2 pad.790
  13.2 0.2 pad.791
  13.4 14.1 %all_gather.14 = f32[4,8,128]{2,1,0:T(8,128)S(1)} all-gather(f32[1,8,128]{2,1,0:T(8,128)S(1)} %slice_add_fusion.40), channel_id=1, replica_groups=mesh['cases'=2,'tm'=4,'region'=4] {'tm'}, dimensions={0}, use_global_device_ids=true | all-gather | bytes 20480 | tf_op jit(solution)/shard_map/all_gather | solution.py:101
  28.1 0.2 pad.226
  28.3 0.2 pad.227
  28.5 13.1 %all_gather.15 = f32[4,8,128]{2,1,0:T(8,128)S(1)} all-gather(f32[1,8,128]{2,1,0:T(8,128)S(1)} %slice_add_fusion.37), channel_id=1, replica_groups=mesh['cases'=2,'tm'=4,'region'=4] {'tm'}, dimensions={0}, use_global_device_ids=true | all-gather | bytes 20480 | tf_op jit(solution)/shard_map/all_gather | solution.py:102
  42.3 0.7 slice-done.1
  43.0 0.7 copy-done.7
  44.5 1.7 %collective-permute-start.3 = (bf16[48,4,128]{2,1,0:T(4,128)(2,1)S(1)}, bf16[48,4,128]{2,1,0:T(4,128)(2,1)S(1)}, u32[]{:S(2)}, u32[]{:S(2)}) collective-permute-start(bf16[48,4,128]{2,1,0:T(4,128)(2,1)S(1)} %get-tuple-element.62), channel_id=1, source_target_pairs={{1,0},{2,1},{3,2},{0,3},{5,4},{6,5},{7,6},{4,7},{9,8},{10,9},{11,1... | collective-permute-start | bytes 147464 | tf_op jit(solution)/shard_map/ppermute | solution.py:20
  46.2 1.8 %collective-permute-done.2 = bf16[48,4,128]{2,1,0:T(4,128)(2,1)S(1)} collective-permute-done((bf16[48,4,128]{2,1,0:T(4,128)(2,1)S(1)}, bf16[48,4,128]{2,1,0:T(4,128)(2,1)S(1)}, u32[]{:S(2)}, u32[]{:S(2)}) %collective-permute-start.2) | collective-permute-done | bytes 49184 | tf_op jit(solution)/shard_map/ppermute | solution.py:17
  48.2 0.6 gather_fusion.1
  48.8 0.5 convolution_bitcast_fusion.1
  52.0 0.2 pad.240
  52.4 13.1 %all_gather.16 = f32[4,8,128]{2,1,0:T(8,128)S(1)} all-gather(f32[1,8,128]{2,1,0:T(8,128)S(1)} %slice_add_fusion.32), channel_id=1, replica_groups=mesh['cases'=2,'tm'=4,'region'=4] {'tm'}, dimensions={0}, use_global_device_ids=true | all-gather | bytes 20480 | tf_op jit(solution)/shard_map/all_gather | solution.py:102
  65.8 0.6 copy-done.4
  67.3 1.7 %collective-permute-start.5 = (bf16[48,4,128]{2,1,0:T(4,128)(2,1)S(1)}, bf16[48,4,128]{2,1,0:T(4,128)(2,1)S(1)}, u32[]{:S(2)}, u32[]{:S(2)}) collective-permute-start(bf16[48,4,128]{2,1,0:T(4,128)(2,1)S(1)} %get-tuple-element.58), channel_id=1, source_target_pairs={{1,0},{2,1},{3,2},{0,3},{5,4},{6,5},{7,6},{4,7},{9,8},{10,9},{11,1... | collective-permute-start | bytes 147464 | tf_op jit(solution)/shard_map/ppermute | solution.py:20
  69.0 1.8 %collective-permute-done.4 = bf16[48,4,128]{2,1,0:T(4,128)(2,1)S(1)} collective-permute-done((bf16[48,4,128]{2,1,0:T(4,128)(2,1)S(1)}, bf16[48,4,128]{2,1,0:T(4,128)(2,1)S(1)}, u32[]{:S(2)}, u32[]{:S(2)}) %collective-permute-start.4) | collective-permute-done | bytes 49184 | tf_op jit(solution)/shard_map/ppermute | solution.py:17
  70.9 0.6 gather_fusion.2
  71.6 0.4 convolution_bitcast_fusion
  75.2 13.1 %all_gather.17 = f32[4,8,128]{2,1,0:T(8,128)S(1)} all-gather(f32[1,8,128]{2,1,0:T(8,128)S(1)} %slice_add_fusion.27), channel_id=1, replica_groups=mesh['cases'=2,'tm'=4,'region'=4] {'tm'}, dimensions={0}, use_global_device_ids=true | all-gather | bytes 20480 | tf_op jit(solution)/shard_map/all_gather | solution.py:102
  89.2 0.8 maximum_add_fusion.2
  (282 shorter events, 14.0 us)
Async XLA Ops:
  0.0 7.3 %copy-start = (bf16[8,4,128,128]{3,2,1,0:T(8,128)(2,1)S(1)}, bf16[8,4,128,128]{3,2,1,0:T(8,128)(2,1)}, u32[]{:S(2)}) copy-start(bf16[8,4,128,128]{3,2,1,0:T(8,128)(2,1)} %param.10) | copy-start | bytes 3145732
  1.1 2.5 %copy-start.8 = (s32[8,64]{1,0:T(8,128)S(1)}, s32[8,64]{1,0:T(8,128)}, u32[]{:S(2)}) copy-start(s32[8,64]{1,0:T(8,128)} %param.14) | copy-start | bytes 6148
  1.1 5.5 %collective-permute-start = (bf16[48,4,128]{2,0,1:T(8,128)(2,1)S(1)}, bf16[48,4,128]{2,0,1:T(8,128)(2,1)S(1)}, u32[]{:S(2)}, u32[]{:S(2)}) collective-permute-start(bf16[48,4,128]{2,0,1:T(8,128)(2,1)S(1)} %get-tuple-element.67), channel_id=1, source_target_pairs={{0,1},{1,2},{2,3},{3,0},{4,5},{5,6},{6,7},{7,4},{8,9},{9,10},{10,1... | collective-permute-start | bytes 147464 | tf_op jit(solution)/shard_map/ppermute | solution.py:17
  1.6 5.0 %collective-permute-start.1 = (bf16[48,4,128]{2,0,1:T(8,128)(2,1)S(1)}, bf16[48,4,128]{2,0,1:T(8,128)(2,1)S(1)}, u32[]{:S(2)}, u32[]{:S(2)}) collective-permute-start(bf16[48,4,128]{2,0,1:T(8,128)(2,1)S(1)} %get-tuple-element.68), channel_id=1, source_target_pairs={{1,0},{2,1},{3,2},{0,3},{5,4},{6,5},{7,6},{4,7},{9,8},{10,9},{11,1... | collective-permute-start | bytes 147464 | tf_op jit(solution)/shard_map/ppermute | solution.py:20
  3.6 0.7 copy-start.9
  4.3 0.7 copy-start.5
  4.3 0.7 copy-start.6
  5.1 0.7 copy-start.10
  5.9 0.7 copy-start.1
  7.8 0.9 copy-start.2
  12.2 0.7 slice-start
  27.5 14.5 %copy-start.3 = (f32[4,8,128]{2,1,0:T(8,128)}, f32[4,8,128]{2,1,0:T(8,128)S(1)}, u32[]{:S(2)}) copy-start(f32[4,8,128]{2,1,0:T(8,128)S(1)} %all_gather.14) | copy-start | bytes 49156
  42.3 0.7 slice-start.1
  43.0 0.7 copy-start.7
  44.4 3.6 %collective-permute-start.2 = (bf16[48,4,128]{2,1,0:T(4,128)(2,1)S(1)}, bf16[48,4,128]{2,1,0:T(4,128)(2,1)S(1)}, u32[]{:S(2)}, u32[]{:S(2)}) collective-permute-start(bf16[48,4,128]{2,1,0:T(4,128)(2,1)S(1)} %get-tuple-element.61), channel_id=1, source_target_pairs={{0,1},{1,2},{2,3},{3,0},{4,5},{5,6},{6,7},{7,4},{8,9},{9,10},{10,1... | collective-permute-start | bytes 147464 | tf_op jit(solution)/shard_map/ppermute | solution.py:17
  44.5 3.5 %collective-permute-start.3 = (bf16[48,4,128]{2,1,0:T(4,128)(2,1)S(1)}, bf16[48,4,128]{2,1,0:T(4,128)(2,1)S(1)}, u32[]{:S(2)}, u32[]{:S(2)}) collective-permute-start(bf16[48,4,128]{2,1,0:T(4,128)(2,1)S(1)} %get-tuple-element.62), channel_id=1, source_target_pairs={{1,0},{2,1},{3,2},{0,3},{5,4},{6,5},{7,6},{4,7},{9,8},{10,9},{11,1... | collective-permute-start | bytes 147464 | tf_op jit(solution)/shard_map/ppermute | solution.py:20
  65.7 0.7 copy-start.4
  67.2 3.6 %collective-permute-start.4 = (bf16[48,4,128]{2,1,0:T(4,128)(2,1)S(1)}, bf16[48,4,128]{2,1,0:T(4,128)(2,1)S(1)}, u32[]{:S(2)}, u32[]{:S(2)}) collective-permute-start(bf16[48,4,128]{2,1,0:T(4,128)(2,1)S(1)} %get-tuple-element.57), channel_id=1, source_target_pairs={{0,1},{1,2},{2,3},{3,0},{4,5},{5,6},{6,7},{7,4},{8,9},{9,10},{10,1... | collective-permute-start | bytes 147464 | tf_op jit(solution)/shard_map/ppermute | solution.py:17
  67.3 3.5 %collective-permute-start.5 = (bf16[48,4,128]{2,1,0:T(4,128)(2,1)S(1)}, bf16[48,4,128]{2,1,0:T(4,128)(2,1)S(1)}, u32[]{:S(2)}, u32[]{:S(2)}) collective-permute-start(bf16[48,4,128]{2,1,0:T(4,128)(2,1)S(1)} %get-tuple-element.58), channel_id=1, source_target_pairs={{1,0},{2,1},{3,2},{0,3},{5,4},{6,5},{7,6},{4,7},{9,8},{10,9},{11,1... | collective-permute-start | bytes 147464 | tf_op jit(solution)/shard_map/ppermute | solution.py:20
where the time goes:
time: 90.4 us; the launch traced here: 90 us
  blocking collectives  53.5 us (59%)
  local copies, waits for them, and re-layouts  12.5 us (14%)
  other arithmetic  11.7 us (13%)
  starting transfers between devices  6.07 us (7%)
  waiting for transfers between devices  3.55 us (4%)
  matrix products  1.36 us (2%)
  between operations  1.28 us (1%)
    all_gather x3, blocking collectives, local(): lax.all_gather(own_map[1][None], 'tm', axis=0, tiled=True)  39.4 us
    all_gather x1, blocking collectives, local(): lax.all_gather(own_map[0][None], 'tm', axis=0, tiled=True)  14.1 us
    unnamed x26, local copies, waits for them, and re-layouts  5.99 us
    ppermute x3, starting transfers between devices, with_halo(): lax.ppermute(lax.slice_in_dim(block, 0, width, axis=dim), axis, backward)  5.45 us
    sub x45, other arithmetic, complex_mul(): first_re * second_re - first_im * second_im  4.13 us
    ppermute x3, waiting for transfers between devices, with_halo(): lax.ppermute(lax.slice_in_dim(block, block.shape[dim] - width, None, axis...  3.54 us
    add x33, other arithmetic, combine(): complex_mul(late[0], early[1]) + late[1]  2.7 us
    pad x34, local copies, waits for them, and re-layouts, local(): lax.associative_scan(combine, (incremental_spin, drive), axis=0)  2.34 us
  transfers between devices with their start and end apart: 6, of which 2 were waited for; matrix products, arithmetic and copies ran while one was open for 0% of the time, Pallas kernels for 0%

commit v1 on v0

--- a/solution.py
+++ b/solution.py
@@ -97,9 +97,25 @@
         drive = input_gain[None] * (drive_base - limit_current(current, saturated_flag[None]))
         local_a, local_b = lax.associative_scan(combine, (incremental_spin, drive), axis=0)
         own_map = (local_a[-1], local_b[-1])
+
+        def change_stops_all_on_mesh(inp, device_axis):
+            fresh = jax.lax.axis_size(device_axis)
+            oldest = jax.lax.axis_index(device_axis)
+            z, block_now = (fresh, oldest)
+            known, state_now = (inp, 1)
+            while state_now < z:
+                lower = jax.lax.ppermute(
+                    known, device_axis, tuple(((no, no ^ state_now) for no in range(z)))
+                )
+                shaped = jnp.concatenate([known, lower], 0)
+                t1 = jnp.concatenate([lower, known], 0)
+                known = jnp.where(block_now & state_now == 0, shaped, t1)
+                state_now = 2 * state_now
+            return known
+
         every_a, every_b = (
             lax.all_gather(own_map[0][None], "tm", axis=0, tiled=True),
-            lax.all_gather(own_map[1][None], "tm", axis=0, tiled=True),
+            change_stops_all_on_mesh(own_map[1][None], "tm"),
         )
         run_a, run_b = lax.associative_scan(combine, (every_a, every_b), axis=0)
         total_a, total_b = (run_a[-1], run_b[-1])

time: 90.4 us -> 73.7 us (0.82)
  blocking collectives: 53.5 us -> 13.3 us
  waiting for transfers between devices: 3.55 us -> 21.4 us
  starting transfers between devices: 6.07 us -> 11.7 us
    all_gather x3 -> x0, blocking collectives: 39.4 us -> none  [local(): lax.all_gather(own_map[1][None], 'tm', axis=0, tiled=True)]
    ppermute x0 -> x6, waiting for transfers between devices: none -> 17.8 us  [change_stops_all_on_mesh(): jax.lax.ppermute(known, device_axis, tuple(((no, no ^ state_now) for no i...]
    ppermute x0 -> x6, starting transfers between devices: none -> 5.64 us  [change_stops_all_on_mesh(): jax.lax.ppermute(known, device_axis, tuple(((no, no ^ state_now) for no i...]
  transfers between devices with their start and end apart: 6 -> 12, of which waited for: 2 -> 7; matrix products, arithmetic and copies ran while one was open for 0% -> 1% of each run, Pallas kernels for 0% -> 0%
where the time goes in v1:
time: 73.7 us; the launch traced here: 73.3 us
  waiting for transfers between devices  21.4 us (29%)
  blocking collectives  13.3 us (18%)
  local copies, waits for them, and re-layouts  12.5 us (17%)
  other arithmetic  11.8 us (16%)
  starting transfers between devices  11.7 us (16%)
  matrix products  1.36 us (2%)
  between operations  1.28 us (2%)
    ppermute x6, waiting for transfers between devices, change_stops_all_on_mesh(): jax.lax.ppermute(known, device_axis, tuple(((no, no ^ state_now) for no i...  17.8 us
    all_gather x1, blocking collectives, local(): lax.all_gather(own_map[0][None], 'tm', axis=0, tiled=True)  13.3 us
    unnamed x26, local copies, waits for them, and re-layouts  5.99 us
    ppermute x6, starting transfers between devices, change_stops_all_on_mesh(): jax.lax.ppermute(known, device_axis, tuple(((no, no ^ state_now) for no i...  5.64 us
    ppermute x3, starting transfers between devices, with_halo(): lax.ppermute(lax.slice_in_dim(block, 0, width, axis=dim), axis, backward)  5.45 us
    sub x45, other arithmetic, complex_mul(): first_re * second_re - first_im * second_im  4.14 us
    ppermute x3, waiting for transfers between devices, with_halo(): lax.ppermute(lax.slice_in_dim(block, block.shape[dim] - width, None, axis...  3.54 us
    add x33, other arithmetic, combine(): complex_mul(late[0], early[1]) + late[1]  2.7 us
  transfers between devices with their start and end apart: 12, of which 7 were waited for; matrix products, arithmetic and copies ran while one was open for 1% of the time, Pallas kernels for 0%

profile of v1, /device:TPU:0, one launch (start us, length us, event | category | flops | bytes accessed | tf_op | source)
XLA Modules:
  0.0 73.3 jit_solution(3225129051459931420)
XLA Ops:
  0.0 1.1 %copy.147 = bf16[48,8,128]{2,0,1:T(8,128)(2,1)S(1)} copy(f32[48,8,128]{2,1,0:T(8,128)} %param.8) | data formatting | bytes 294912 | tf_op args[0]
  1.1 0.5 collective-permute-start
  1.6 2.0 %collective-permute-start.1 = (bf16[48,4,128]{2,0,1:T(8,128)(2,1)S(1)}, bf16[48,4,128]{2,0,1:T(8,128)(2,1)S(1)}, u32[]{:S(2)}, u32[]{:S(2)}) collective-permute-start(bf16[48,4,128]{2,0,1:T(8,128)(2,1)S(1)} %get-tuple-element.68), channel_id=1, source_target_pairs={{1,0},{2,1},{3,2},{0,3},{5,4},{6,5},{7,6},{4,7},{9,8},{10,9},{11,1... | collective-permute-start | bytes 147464 | tf_op jit(solution)/shard_map/ppermute | solution.py:20
  3.6 0.7 copy-done.9
  4.5 0.5 copy-done.5
  5.1 0.7 copy-done.10
  5.9 0.6 copy-done.1
  6.6 0.6 gather_fusion
  8.0 0.7 %copy-done.2 = bf16[48,8,128]{2,1,0:T(8,128)(2,1)S(1)} copy-done((bf16[48,8,128]{2,1,0:T(8,128)(2,1)S(1)}, bf16[48,8,128]{2,1,0:T(8,128)(2,1)}, u32[]{:S(2)}) %copy-start.2) | copy-done | bytes 98328
  12.9 0.5 slice-done
  14.4 2.4 %collective-permute-start.2 = (f32[1,8,128]{2,1,0:T(8,128)S(1)}, f32[1,8,128]{2,1,0:T(8,128)S(1)}, u32[]{:S(2)}, u32[]{:S(2)}) collective-permute-start(f32[1,8,128]{2,1,0:T(8,128)S(1)} %slice_add_fusion.37), channel_id=1, source_target_pairs={{0,4},{4,0},{8,12},{12,8},{1,5},{5,1},{9,13},{13,9},{2,6},{6,2},{1... | collective-permute-start | bytes 12296 | tf_op jit(solution)/shard_map/ppermute | solution.py:107
  16.8 13.3 %all_gather.2 = f32[4,8,128]{2,1,0:T(8,128)S(1)} all-gather(f32[1,8,128]{2,1,0:T(8,128)S(1)} %slice_add_fusion.40), channel_id=1, replica_groups=mesh['cases'=2,'tm'=4,'region'=4] {'tm'}, dimensions={0}, use_global_device_ids=true | all-gather | bytes 20480 | tf_op jit(solution)/shard_map/all_gather | solution.py:117
  30.1 0.6 collective-permute-start.3
  30.8 4.0 %collective-permute-done.3 = f32[2,8,128]{2,1,0:T(8,128)S(1)} collective-permute-done((f32[2,8,128]{2,1,0:T(8,128)S(1)}, f32[2,8,128]{2,1,0:T(8,128)S(1)}, u32[]{:S(2)}, u32[]{:S(2)}) %collective-permute-start.3) | collective-permute-done | bytes 8224 | tf_op jit(solution)/shard_map/ppermute | solution.py:107
  35.4 0.7 slice-done.1
  36.2 0.7 copy-done.7
  37.6 1.7 %collective-permute-start.5 = (bf16[48,4,128]{2,1,0:T(4,128)(2,1)S(1)}, bf16[48,4,128]{2,1,0:T(4,128)(2,1)S(1)}, u32[]{:S(2)}, u32[]{:S(2)}) collective-permute-start(bf16[48,4,128]{2,1,0:T(4,128)(2,1)S(1)} %get-tuple-element.62), channel_id=1, source_target_pairs={{1,0},{2,1},{3,2},{0,3},{5,4},{6,5},{7,6},{4,7},{9,8},{10,9},{11,1... | collective-permute-start | bytes 147464 | tf_op jit(solution)/shard_map/ppermute | solution.py:20
  39.3 1.8 %collective-permute-done.4 = bf16[48,4,128]{2,1,0:T(4,128)(2,1)S(1)} collective-permute-done((bf16[48,4,128]{2,1,0:T(4,128)(2,1)S(1)}, bf16[48,4,128]{2,1,0:T(4,128)(2,1)S(1)}, u32[]{:S(2)}, u32[]{:S(2)}) %collective-permute-start.4) | collective-permute-done | bytes 49184 | tf_op jit(solution)/shard_map/ppermute | solution.py:17
  41.3 0.6 gather_fusion.1
  45.5 0.5 collective-permute-start.6
  46.0 3.2 %collective-permute-done.6 = f32[1,8,128]{2,1,0:T(8,128)S(1)} collective-permute-done((f32[1,8,128]{2,1,0:T(8,128)S(1)}, f32[1,8,128]{2,1,0:T(8,128)S(1)}, u32[]{:S(2)}, u32[]{:S(2)}) %collective-permute-start.6) | collective-permute-done | bytes 4128 | tf_op jit(solution)/shard_map/ppermute | solution.py:107
  49.2 0.8 %collective-permute-start.7 = (f32[2,8,128]{2,1,0:T(8,128)S(1)}, f32[2,8,128]{2,1,0:T(8,128)S(1)}, u32[]{:S(2)}, u32[]{:S(2)}) collective-permute-start(f32[2,8,128]{2,1,0:T(8,128)S(1)} %maximum_select_fusion.4), channel_id=1, source_target_pairs={{0,8},{4,12},{8,0},{12,4},{1,9},{5,13},{9,1},{13,5},{2,10},{6,14},... | collective-permute-start | bytes 24584 | tf_op jit(solution)/shard_map/ppermute | solution.py:107
  50.0 3.8 %collective-permute-done.7 = f32[2,8,128]{2,1,0:T(8,128)S(1)} collective-permute-done((f32[2,8,128]{2,1,0:T(8,128)S(1)}, f32[2,8,128]{2,1,0:T(8,128)S(1)}, u32[]{:S(2)}, u32[]{:S(2)}) %collective-permute-start.7) | collective-permute-done | bytes 8224 | tf_op jit(solution)/shard_map/ppermute | solution.py:107
  54.1 0.6 copy-done.4
  55.5 1.7 %collective-permute-start.9 = (bf16[48,4,128]{2,1,0:T(4,128)(2,1)S(1)}, bf16[48,4,128]{2,1,0:T(4,128)(2,1)S(1)}, u32[]{:S(2)}, u32[]{:S(2)}) collective-permute-start(bf16[48,4,128]{2,1,0:T(4,128)(2,1)S(1)} %get-tuple-element.58), channel_id=1, source_target_pairs={{1,0},{2,1},{3,2},{0,3},{5,4},{6,5},{7,6},{4,7},{9,8},{10,9},{11,1... | collective-permute-start | bytes 147464 | tf_op jit(solution)/shard_map/ppermute | solution.py:20
  57.2 1.8 %collective-permute-done.8 = bf16[48,4,128]{2,1,0:T(4,128)(2,1)S(1)} collective-permute-done((bf16[48,4,128]{2,1,0:T(4,128)(2,1)S(1)}, bf16[48,4,128]{2,1,0:T(4,128)(2,1)S(1)}, u32[]{:S(2)}, u32[]{:S(2)}) %collective-permute-start.8) | collective-permute-done | bytes 49184 | tf_op jit(solution)/shard_map/ppermute | solution.py:17
  59.2 0.6 gather_fusion.2
  63.4 0.5 collective-permute-start.10
  63.9 3.2 %collective-permute-done.10 = f32[1,8,128]{2,1,0:T(8,128)S(1)} collective-permute-done((f32[1,8,128]{2,1,0:T(8,128)S(1)}, f32[1,8,128]{2,1,0:T(8,128)S(1)}, u32[]{:S(2)}, u32[]{:S(2)}) %collective-permute-start.10) | collective-permute-done | bytes 4128 | tf_op jit(solution)/shard_map/ppermute | solution.py:107
  67.1 0.8 %collective-permute-start.11 = (f32[2,8,128]{2,1,0:T(8,128)S(1)}, f32[2,8,128]{2,1,0:T(8,128)S(1)}, u32[]{:S(2)}, u32[]{:S(2)}) collective-permute-start(f32[2,8,128]{2,1,0:T(8,128)S(1)} %maximum_select_fusion.5), channel_id=1, source_target_pairs={{0,8},{4,12},{8,0},{12,4},{1,9},{5,13},{9,1},{13,5},{2,10},{6,14},... | collective-permute-start | bytes 24584 | tf_op jit(solution)/shard_map/ppermute | solution.py:107
  67.9 3.8 %collective-permute-done.11 = f32[2,8,128]{2,1,0:T(8,128)S(1)} collective-permute-done((f32[2,8,128]{2,1,0:T(8,128)S(1)}, f32[2,8,128]{2,1,0:T(8,128)S(1)}, u32[]{:S(2)}, u32[]{:S(2)}) %collective-permute-start.11) | collective-permute-done | bytes 8224 | tf_op jit(solution)/shard_map/ppermute | solution.py:107
  72.5 0.8 %maximum_add_fusion.2 = f32[48,8,128]{2,1,0:T(8,128)} fusion(f32[48,8,64]{2,1,0:T(8,128)S(1)} %get-tuple-element.26, f32[48,8,64]{2,1,0:T(8,128)S(1)} %get-tuple-element.25, f32[48,8,128]{2,1,0:T(8,128)S(1)} %pad.254, f32[48,8,128]{2,1,0:T(8,128)S(1)} %pad.255), kind=kLoop, calls=%fused_computation.44 | loop fusion | flops 147456 | bytes 786432 | tf_op jit(solution)/shard_map/add | solution.py:132
  (297 shorter events, 16.3 us)
Async XLA Ops:
  0.0 7.3 %copy-start = (bf16[8,4,128,128]{3,2,1,0:T(8,128)(2,1)S(1)}, bf16[8,4,128,128]{3,2,1,0:T(8,128)(2,1)}, u32[]{:S(2)}) copy-start(bf16[8,4,128,128]{3,2,1,0:T(8,128)(2,1)} %param.10) | copy-start | bytes 3145732
  1.1 2.5 %copy-start.8 = (s32[8,64]{1,0:T(8,128)S(1)}, s32[8,64]{1,0:T(8,128)}, u32[]{:S(2)}) copy-start(s32[8,64]{1,0:T(8,128)} %param.14) | copy-start | bytes 6148
  1.1 5.5 %collective-permute-start = (bf16[48,4,128]{2,0,1:T(8,128)(2,1)S(1)}, bf16[48,4,128]{2,0,1:T(8,128)(2,1)S(1)}, u32[]{:S(2)}, u32[]{:S(2)}) collective-permute-start(bf16[48,4,128]{2,0,1:T(8,128)(2,1)S(1)} %get-tuple-element.67), channel_id=1, source_target_pairs={{0,1},{1,2},{2,3},{3,0},{4,5},{5,6},{6,7},{7,4},{8,9},{9,10},{10,1... | collective-permute-start | bytes 147464 | tf_op jit(solution)/shard_map/ppermute | solution.py:17
  1.6 5.0 %collective-permute-start.1 = (bf16[48,4,128]{2,0,1:T(8,128)(2,1)S(1)}, bf16[48,4,128]{2,0,1:T(8,128)(2,1)S(1)}, u32[]{:S(2)}, u32[]{:S(2)}) collective-permute-start(bf16[48,4,128]{2,0,1:T(8,128)(2,1)S(1)} %get-tuple-element.68), channel_id=1, source_target_pairs={{1,0},{2,1},{3,2},{0,3},{5,4},{6,5},{7,6},{4,7},{9,8},{10,9},{11,1... | collective-permute-start | bytes 147464 | tf_op jit(solution)/shard_map/ppermute | solution.py:20
  3.6 0.7 copy-start.9
  4.3 0.7 copy-start.5
  4.3 0.7 copy-start.6
  5.1 0.7 copy-start.10
  5.9 0.7 copy-start.1
  7.8 0.9 %copy-start.2 = (bf16[48,8,128]{2,1,0:T(8,128)(2,1)S(1)}, bf16[48,8,128]{2,1,0:T(8,128)(2,1)}, u32[]{:S(2)}) copy-start(bf16[48,8,128]{2,1,0:T(8,128)(2,1)} %param.9) | copy-start | bytes 294916
  12.7 0.7 slice-start
  14.4 15.7 %collective-permute-start.2 = (f32[1,8,128]{2,1,0:T(8,128)S(1)}, f32[1,8,128]{2,1,0:T(8,128)S(1)}, u32[]{:S(2)}, u32[]{:S(2)}) collective-permute-start(f32[1,8,128]{2,1,0:T(8,128)S(1)} %slice_add_fusion.37), channel_id=1, source_target_pairs={{0,4},{4,0},{8,12},{12,8},{1,5},{5,1},{9,13},{13,9},{2,6},{6,2},{1... | collective-permute-start | bytes 12296 | tf_op jit(solution)/shard_map/ppermute | solution.py:107
  30.1 5.0 %copy-start.3 = (f32[4,8,128]{2,1,0:T(8,128)}, f32[4,8,128]{2,1,0:T(8,128)S(1)}, u32[]{:S(2)}) copy-start(f32[4,8,128]{2,1,0:T(8,128)S(1)} %all_gather.2) | copy-start | bytes 49156
  30.1 4.6 %collective-permute-start.3 = (f32[2,8,128]{2,1,0:T(8,128)S(1)}, f32[2,8,128]{2,1,0:T(8,128)S(1)}, u32[]{:S(2)}, u32[]{:S(2)}) collective-permute-start(f32[2,8,128]{2,1,0:T(8,128)S(1)} %maximum_select_fusion.3), channel_id=1, source_target_pairs={{0,8},{4,12},{8,0},{12,4},{1,9},{5,13},{9,1},{13,5},{2,10},{6,14},... | collective-permute-start | bytes 24584 | tf_op jit(solution)/shard_map/ppermute | solution.py:107
  35.4 0.7 slice-start.1
  36.2 0.7 copy-start.7
  37.5 3.6 %collective-permute-start.4 = (bf16[48,4,128]{2,1,0:T(4,128)(2,1)S(1)}, bf16[48,4,128]{2,1,0:T(4,128)(2,1)S(1)}, u32[]{:S(2)}, u32[]{:S(2)}) collective-permute-start(bf16[48,4,128]{2,1,0:T(4,128)(2,1)S(1)} %get-tuple-element.61), channel_id=1, source_target_pairs={{0,1},{1,2},{2,3},{3,0},{4,5},{5,6},{6,7},{7,4},{8,9},{9,10},{10,1... | collective-permute-start | bytes 147464 | tf_op jit(solution)/shard_map/ppermute | solution.py:17
  37.6 3.5 %collective-permute-start.5 = (bf16[48,4,128]{2,1,0:T(4,128)(2,1)S(1)}, bf16[48,4,128]{2,1,0:T(4,128)(2,1)S(1)}, u32[]{:S(2)}, u32[]{:S(2)}) collective-permute-start(bf16[48,4,128]{2,1,0:T(4,128)(2,1)S(1)} %get-tuple-element.62), channel_id=1, source_target_pairs={{1,0},{2,1},{3,2},{0,3},{5,4},{6,5},{7,6},{4,7},{9,8},{10,9},{11,1... | collective-permute-start | bytes 147464 | tf_op jit(solution)/shard_map/ppermute | solution.py:20
  45.5 3.7 %collective-permute-start.6 = (f32[1,8,128]{2,1,0:T(8,128)S(1)}, f32[1,8,128]{2,1,0:T(8,128)S(1)}, u32[]{:S(2)}, u32[]{:S(2)}) collective-permute-start(f32[1,8,128]{2,1,0:T(8,128)S(1)} %slice_add_fusion.32), channel_id=1, source_target_pairs={{0,4},{4,0},{8,12},{12,8},{1,5},{5,1},{9,13},{13,9},{2,6},{6,2},{1... | collective-permute-start | bytes 12296 | tf_op jit(solution)/shard_map/ppermute | solution.py:107
  49.2 4.5 %collective-permute-start.7 = (f32[2,8,128]{2,1,0:T(8,128)S(1)}, f32[2,8,128]{2,1,0:T(8,128)S(1)}, u32[]{:S(2)}, u32[]{:S(2)}) collective-permute-start(f32[2,8,128]{2,1,0:T(8,128)S(1)} %maximum_select_fusion.4), channel_id=1, source_target_pairs={{0,8},{4,12},{8,0},{12,4},{1,9},{5,13},{9,1},{13,5},{2,10},{6,14},... | collective-permute-start | bytes 24584 | tf_op jit(solution)/shard_map/ppermute | solution.py:107
  54.0 0.7 copy-start.4
  55.4 3.6 %collective-permute-start.8 = (bf16[48,4,128]{2,1,0:T(4,128)(2,1)S(1)}, bf16[48,4,128]{2,1,0:T(4,128)(2,1)S(1)}, u32[]{:S(2)}, u32[]{:S(2)}) collective-permute-start(bf16[48,4,128]{2,1,0:T(4,128)(2,1)S(1)} %get-tuple-element.57), channel_id=1, source_target_pairs={{0,1},{1,2},{2,3},{3,0},{4,5},{5,6},{6,7},{7,4},{8,9},{9,10},{10,1... | collective-permute-start | bytes 147464 | tf_op jit(solution)/shard_map/ppermute | solution.py:17
  55.5 3.5 %collective-permute-start.9 = (bf16[48,4,128]{2,1,0:T(4,128)(2,1)S(1)}, bf16[48,4,128]{2,1,0:T(4,128)(2,1)S(1)}, u32[]{:S(2)}, u32[]{:S(2)}) collective-permute-start(bf16[48,4,128]{2,1,0:T(4,128)(2,1)S(1)} %get-tuple-element.58), channel_id=1, source_target_pairs={{1,0},{2,1},{3,2},{0,3},{5,4},{6,5},{7,6},{4,7},{9,8},{10,9},{11,1... | collective-permute-start | bytes 147464 | tf_op jit(solution)/shard_map/ppermute | solution.py:20
  63.4 3.7 %collective-permute-start.10 = (f32[1,8,128]{2,1,0:T(8,128)S(1)}, f32[1,8,128]{2,1,0:T(8,128)S(1)}, u32[]{:S(2)}, u32[]{:S(2)}) collective-permute-start(f32[1,8,128]{2,1,0:T(8,128)S(1)} %slice_add_fusion.27), channel_id=1, source_target_pairs={{0,4},{4,0},{8,12},{12,8},{1,5},{5,1},{9,13},{13,9},{2,6},{6,2},{1... | collective-permute-start | bytes 12296 | tf_op jit(solution)/shard_map/ppermute | solution.py:107
  67.1 4.5 %collective-permute-start.11 = (f32[2,8,128]{2,1,0:T(8,128)S(1)}, f32[2,8,128]{2,1,0:T(8,128)S(1)}, u32[]{:S(2)}, u32[]{:S(2)}) collective-permute-start(f32[2,8,128]{2,1,0:T(8,128)S(1)} %maximum_select_fusion.5), channel_id=1, source_target_pairs={{0,8},{4,12},{8,0},{12,4},{1,9},{5,13},{9,1},{13,5},{2,10},{6,14},... | collective-permute-start | bytes 24584 | tf_op jit(solution)/shard_map/ppermute | solution.py:107
